TPU v7x, 32 devices: a whole 2x2x4 slice. The times are simulated.
32 devices in a mesh: span: 8 (over z, x), chord: 4 (over y, core).
Axes of the slice: x: 2, y: 2, z: 4, core: 2. Of those that a mesh axis runs over, the one named last changes fastest.
Arguments:
- displacement: bfloat16 [8, 4, 1024, 128], P('span', 'chord'), may hold values from -12 to 12
- packed_blocks: bfloat16 [8, 4, 1024, 1024], P('span', 'chord'), as said below
- flex_scale: float32 [8, 4, 1024], P('span', 'chord'), may hold values from 0.5 to 2
- dirichlet_scale: float32 [8, 4, 1024], P('span', 'chord'), may hold values from 0.5 to 2
- dirichlet_diag: bfloat16 [8, 4, 1024], P('span', 'chord'), may hold values from 1.1953125 to 2.5
- link_rows: int32 [8, 4, 4, 256], P('span', 'chord'), may hold values from 0 to 1023, as said below
- link_signs: int32 [8, 4, 4, 256], P('span', 'chord'), may hold values from -1 to 1, as said below
- link_counts: int32 [8, 4, 4], P('span', 'chord'), may hold values from 0 to 256, as said below
Outputs:
- multipliers: float32 [8, 4, 1024, 128], P('span', 'chord')
- residual: float32 [8, 4, 1024, 128], P('span', 'chord')
Inputs may be any that keep to these rules, and one draw needn't show every extreme that they name: `link_rows`: for each subdomain the 4 x 256 entries name every row 0 to 1023 exactly once. `link_counts`: each count equals the count of the opposite direction on the neighbour's side; it is 0 at the edges of the mesh and toward unlisted neighbours, otherwise at least 64; some subdomain uses all 256 slots toward a span neighbour and some toward a chord neighbour. `link_signs`: every entry is 1 or -1; slot p toward a neighbour holds the opposite sign of slot p of the opposite direction on that neighbour. `packed_blocks`: each block's diagonal lies between 1.2 and 2.5.
All inputs are finite; a program needn't handle non-finite values.
Results may differ from a plain program's by a relative error of at most 0.0065.
Values may be sent and summed in bfloat16 or wider, within the bound.
A program may use at most 64 MiB of HBM per device.

v0:
```python
import jax
import jax.numpy as jnp
from jax import lax
from jax.sharding import PartitionSpec as P


def extended(block, sides, width):
    for axis, dim in sides:
        count = lax.axis_size(axis)
        forward = [(i, i + 1) for i in range(count - 1)]
        backward = [(target, source) for source, target in forward]
        low = lax.ppermute(
            lax.slice_in_dim(block, block.shape[dim] - width, None, axis=dim), axis, forward
        )
        high = lax.ppermute(lax.slice_in_dim(block, 0, width, axis=dim), axis, backward)
        block = jnp.concatenate([low, block, high], axis=dim)
    return block


def build_blocks(packed, diag):
    size = packed.shape[0]
    row_ids = lax.broadcasted_iota(jnp.int32, (size, size), 0)
    col_ids = lax.broadcasted_iota(jnp.int32, (size, size), 1)
    mirror = packed.T
    flex_block = jnp.where(col_ids >= row_ids, packed, mirror)
    lower = jnp.where(row_ids > col_ids, packed, mirror)
    dirichlet_block = jnp.where(row_ids == col_ids, diag[:, None], lower)
    return (flex_block, dirichlet_block)


def local_term(block, scale, sign_row, field):
    operand = (scale[:, None] * sign_row[:, None] * field).astype(jnp.bfloat16)
    product = jnp.dot(block, operand, preferred_element_type=jnp.float32)
    return (sign_row[:, None] * scale[:, None] * product).astype(jnp.bfloat16)


def exchange_rows(term, flat_rows, valid, slots):
    width = term.shape[1]
    sent = jnp.take(term, flat_rows, axis=0).reshape(4, slots, width)
    sent = jnp.where(valid[:, :, None], sent, jnp.zeros_like(sent))
    span_in = extended(sent[0:2], (("span", 0),), 1)
    chord_in = extended(sent[2:4], (("chord", 0),), 1)
    received = jnp.stack([span_in[0], span_in[3], chord_in[0], chord_in[3]])
    received = jnp.where(valid[:, :, None], received, jnp.zeros_like(received))
    total = sent.astype(jnp.float32) + received.astype(jnp.float32)
    return (
        jnp.zeros((term.shape[0], width), jnp.float32)
        .at[flat_rows]
        .set(total.reshape(4 * slots, width))
    )


def local_gram(left, right):
    return lax.dot_general(
        left,
        right,
        (((0,), (0,)), ((), ())),
        precision=lax.Precision.HIGHEST,
        preferred_element_type=jnp.float32,
    )


def gram(left, right):
    return 0.5 * lax.psum(local_gram(left, right), ("span", "chord"))


def spd_solve(matrix, rhs):
    factor = jnp.linalg.cholesky(matrix)
    return jax.scipy.linalg.cho_solve((factor, True), rhs)


def mat_right(field, small):
    return jnp.dot(
        field, small, precision=lax.Precision.HIGHEST, preferred_element_type=jnp.float32
    )


def shards(
    displacement,
    packed_blocks,
    flex_scale,
    dirichlet_scale,
    dirichlet_diag,
    link_rows,
    link_signs,
    link_counts,
):
    rows_local = link_rows[0, 0]
    slots = rows_local.shape[1]
    flat_rows = rows_local.reshape(-1)
    valid = lax.broadcasted_iota(jnp.int32, rows_local.shape, 1) < link_counts[0, 0][:, None]
    sign_values = jnp.where(valid, link_signs[0, 0], 0).astype(jnp.float32).reshape(-1)
    sign_row = jnp.zeros((packed_blocks.shape[2],), jnp.float32).at[flat_rows].set(sign_values)
    flex_block, dirichlet_block = build_blocks(packed_blocks[0, 0], dirichlet_diag[0, 0])
    fscale = flex_scale[0, 0]
    dscale = dirichlet_scale[0, 0]
    gap_term = (sign_row[:, None] * displacement[0, 0].astype(jnp.float32)).astype(jnp.bfloat16)
    right = exchange_rows(gap_term, flat_rows, valid, slots)
    residual = right
    precond = exchange_rows(
        local_term(dirichlet_block, dscale, sign_row, residual), flat_rows, valid, slots
    )
    gamma = gram(precond, residual)
    image = exchange_rows(
        local_term(flex_block, fscale, sign_row, precond), flat_rows, valid, slots
    )
    curv = gram(precond, image)
    alpha = spd_solve(curv, gamma)
    multipliers = mat_right(precond, alpha)
    residual = residual - mat_right(image, alpha)
    return (multipliers[None, None], residual[None, None])


def solution(mesh):
    return jax.shard_map(
        shards,
        mesh=mesh,
        in_specs=(
            P("span", "chord", None, None),
            P("span", "chord", None, None),
            P("span", "chord", None),
            P("span", "chord", None),
            P("span", "chord", None),
            P("span", "chord", None, None),
            P("span", "chord", None, None),
            P("span", "chord", None),
        ),
        out_specs=(P("span", "chord", None, None), P("span", "chord", None, None)),
        check_vma=False,
    )
```

profile of v0, /device:TPU:0, one launch (start us, length us, event | category | flops | bytes accessed | tf_op | source)
XLA Modules:
  0.0 250.4 jit_solution(7497413267375621931)
XLA Ops:
  10.1 4.3 %scatter_custom_fusion = f32[1024]{0:T(1024)S(1)} fusion(s32[1024]{0:T(1024)S(1)} %bitcast.88, f32[1024]{0:T(1024)S(1)} %select_convert_fusion, f32[]{:T(128)} %constant.62.clone.1), kind=kCustom, calls=%fused_computation.86 | custom fusion | bytes 4100 | tf_op jit(solution)/shard_map/scatter | solution.py:93
  15.6 3.2 %gather_fusion = bf16[1024,128]{1,0:T(8,128)(2,1)S(1)} fusion(bf16[1024,128]{1,0:T(8,128)(2,1)S(1)} %fusion.22, s32[1024]{0:T(1024)S(1)} %fusion.57), kind=kCustom, calls=%fused_computation.clone | custom fusion | bytes 528384 | tf_op jit(solution)/shard_map/jit(_take)/gather | solution.py:39
  19.2 4.8 %collective-permute-start = (bf16[1,256,128]{2,1,0:T(8,128)(2,1)S(1)}, bf16[1,256,128]{2,1,0:T(8,128)(2,1)S(1)}, u32[]{:S(2)}, u32[]{:S(2)}) collective-permute-start(bf16[1,256,128]{2,1,0:T(8,128)(2,1)S(1)} %get-tuple-element.13), channel_id=1, source_target_pairs={{0,4},{4,8},{8,12},{12,16},{16,20},{20,24},{24,28},{1,5},{5,9},{9,... | collective-permute-start | bytes 196616 | tf_op jit(solution)/shard_map/ppermute | solution.py:12
  25.4 3.0 %collective-permute-start.2 = (bf16[1,256,128]{2,1,0:T(8,128)(2,1)S(1)}, bf16[1,256,128]{2,1,0:T(8,128)(2,1)S(1)}, u32[]{:S(2)}, u32[]{:S(2)}) collective-permute-start(bf16[1,256,128]{2,1,0:T(8,128)(2,1)S(1)} %get-tuple-element.15), channel_id=1, source_target_pairs={{0,1},{1,2},{2,3},{4,5},{5,6},{6,7},{8,9},{9,10},{10,11},{12,13},{... | collective-permute-start | bytes 196616 | tf_op jit(solution)/shard_map/ppermute | solution.py:12
  29.8 2.6 %copy.10 = bf16[1024,1024]{0,1:T(8,128)(2,1)} copy(bf16[1024,1024]{1,0:T(8,128)(2,1)S(1)} %bitcast.76) | data formatting | bytes 4194304 | tf_op jit(solution)/shard_map/squeeze | solution.py:94
  32.4 2.7 %collective-permute-done.1 = bf16[1,256,128]{2,1,0:T(8,128)(2,1)S(1)} collective-permute-done((bf16[1,256,128]{2,1,0:T(8,128)(2,1)S(1)}, bf16[1,256,128]{2,1,0:T(8,128)(2,1)S(1)}, u32[]{:S(2)}, u32[]{:S(2)}) %collective-permute-start.1) | collective-permute-done | bytes 65568 | tf_op jit(solution)/shard_map/ppermute | solution.py:15
  35.4 4.0 %scatter_custom_fusion.1 = f32[1024,128]{1,0:T(8,128)S(1)} fusion(s32[1024]{0:T(1024)S(1)} %bitcast.89, bf16[1024,128]{1,0:T(8,128)(2,1)S(1)} %bitcast_select_fusion.2, f32[]{:T(128)} %constant.62.clone.1, pred[1024]{0:T(1024)(128)(4,1)S(1)} %lt.42, bf16[]{:T(256)} %constant.65.clone.1, bf16[1024,128]{1,0:T(8,128)(2,1)S(1)} %gather_fusion, ...), kind=kCustom, calls=%fused_computation.36 | custom fusion | flops 655360 | bytes 1050630 | tf_op jit(solution)/shard_map/scatter | solution.py:49
  39.3 2.4 fusion.18
  41.8 3.2 %gather_fusion.1 = bf16[1024,128]{1,0:T(8,128)(2,1)S(1)} fusion(bf16[1024,128]{1,0:T(8,128)(2,1)S(1)} %fusion.18, s32[1024]{0:T(1024)S(1)} %fusion.57), kind=kCustom, calls=%fused_computation.1.clone | custom fusion | bytes 528384 | tf_op jit(solution)/shard_map/jit(_take)/gather | solution.py:39
  45.4 4.3 %collective-permute-start.4 = (bf16[1,256,128]{2,1,0:T(8,128)(2,1)S(1)}, bf16[1,256,128]{2,1,0:T(8,128)(2,1)S(1)}, u32[]{:S(2)}, u32[]{:S(2)}) collective-permute-start(bf16[1,256,128]{2,1,0:T(8,128)(2,1)S(1)} %get-tuple-element.9), channel_id=1, source_target_pairs={{0,4},{4,8},{8,12},{12,16},{16,20},{20,24},{24,28},{1,5},{5,9},{9,... | collective-permute-start | bytes 196616 | tf_op jit(solution)/shard_map/ppermute | solution.py:12
  51.1 3.0 %collective-permute-start.6 = (bf16[1,256,128]{2,1,0:T(8,128)(2,1)S(1)}, bf16[1,256,128]{2,1,0:T(8,128)(2,1)S(1)}, u32[]{:S(2)}, u32[]{:S(2)}) collective-permute-start(bf16[1,256,128]{2,1,0:T(8,128)(2,1)S(1)} %get-tuple-element.11), channel_id=1, source_target_pairs={{0,1},{1,2},{2,3},{4,5},{5,6},{6,7},{8,9},{9,10},{10,11},{12,13},{... | collective-permute-start | bytes 196616 | tf_op jit(solution)/shard_map/ppermute | solution.py:12
  55.5 5.4 %collective-permute-done.5 = bf16[1,256,128]{2,1,0:T(8,128)(2,1)S(1)} collective-permute-done((bf16[1,256,128]{2,1,0:T(8,128)(2,1)S(1)}, bf16[1,256,128]{2,1,0:T(8,128)(2,1)S(1)}, u32[]{:S(2)}, u32[]{:S(2)}) %collective-permute-start.5) | collective-permute-done | bytes 65568 | tf_op jit(solution)/shard_map/ppermute | solution.py:15
  61.8 4.3 %scatter_custom_fusion.2 = f32[1024,128]{1,0:T(8,128)S(1)} fusion(s32[1024]{0:T(1024)S(1)} %bitcast.90, bf16[1024,128]{1,0:T(8,128)(2,1)} %bitcast_select_fusion.1, f32[]{:T(128)} %constant.62.clone.1, pred[1024]{0:T(1024)(128)(4,1)S(1)} %lt.42, bf16[]{:T(256)} %constant.65.clone.1, bf16[1024,128]{1,0:T(8,128)(2,1)S(1)} %gather_fusion.1, ...), kind=kCustom, calls=%fused_computation.31 | custom fusion | flops 655360 | bytes 1050630 | tf_op jit(solution)/shard_map/scatter | solution.py:49
  66.1 2.4 fusion.15
  68.5 3.2 %gather_fusion.2 = bf16[1024,128]{1,0:T(8,128)(2,1)S(1)} fusion(bf16[1024,128]{1,0:T(8,128)(2,1)S(1)} %fusion.15, s32[1024]{0:T(1024)S(1)} %fusion.57), kind=kCustom, calls=%fused_computation.2.clone | custom fusion | bytes 528384 | tf_op jit(solution)/shard_map/jit(_take)/gather | solution.py:39
  72.2 3.3 %collective-permute-start.8 = (bf16[1,256,128]{2,1,0:T(8,128)(2,1)S(1)}, bf16[1,256,128]{2,1,0:T(8,128)(2,1)S(1)}, u32[]{:S(2)}, u32[]{:S(2)}) collective-permute-start(bf16[1,256,128]{2,1,0:T(8,128)(2,1)S(1)} %get-tuple-element.5), channel_id=1, source_target_pairs={{0,4},{4,8},{8,12},{12,16},{16,20},{20,24},{24,28},{1,5},{5,9},{9,... | collective-permute-start | bytes 196616 | tf_op jit(solution)/shard_map/ppermute | solution.py:12
  76.8 3.0 %collective-permute-start.10 = (bf16[1,256,128]{2,1,0:T(8,128)(2,1)S(1)}, bf16[1,256,128]{2,1,0:T(8,128)(2,1)S(1)}, u32[]{:S(2)}, u32[]{:S(2)}) collective-permute-start(bf16[1,256,128]{2,1,0:T(8,128)(2,1)S(1)} %get-tuple-element.7), channel_id=1, source_target_pairs={{0,1},{1,2},{2,3},{4,5},{5,6},{6,7},{8,9},{9,10},{10,11},{12,13},{... | collective-permute-start | bytes 196616 | tf_op jit(solution)/shard_map/ppermute | solution.py:12
  81.3 1.6 fusion.68
  83.0 3.6 %collective-permute-done.9 = bf16[1,256,128]{2,1,0:T(8,128)(2,1)S(1)} collective-permute-done((bf16[1,256,128]{2,1,0:T(8,128)(2,1)S(1)}, bf16[1,256,128]{2,1,0:T(8,128)(2,1)S(1)}, u32[]{:S(2)}, u32[]{:S(2)}) %collective-permute-start.9) | collective-permute-done | bytes 65568 | tf_op jit(solution)/shard_map/ppermute | solution.py:15
  86.9 4.0 %scatter_custom_fusion.3 = f32[1024,128]{1,0:T(8,128)S(1)} fusion(s32[1024]{0:T(1024)S(1)} %bitcast.91, bf16[1024,128]{1,0:T(8,128)(2,1)S(1)} %bitcast_select_fusion, f32[]{:T(128)} %constant.62.clone.1, pred[1024]{0:T(1024)(128)(4,1)S(1)} %lt.42, bf16[]{:T(256)} %constant.65.clone.1, bf16[1024,128]{1,0:T(8,128)(2,1)S(1)} %gather_fusion.2, ...), kind=kCustom, calls=%fused_computation.26 | custom fusion | flops 655360 | bytes 1050630 | tf_op jit(solution)/shard_map/scatter | solution.py:49
  90.8 1.6 fusion.67
  92.5 122.3 %all-reduce.3.cloned.1.call-done = (f32[128,128]{1,0:T(8,128)}, f32[128,128]{1,0:T(8,128)}) async-done(((f32[128,128]{1,0:T(8,128)}, f32[128,128]{1,0:T(8,128)}), (f32[128,128]{1,0:T(8,128)}, f32[128,128]{1,0:T(8,128)})) %all-reduce.3.cloned.1.call-update) | async-done | bytes 131088 | tf_op jit(solution)/shard_map/psum | solution.py:64
  216.6 11.7 %cholesky.16 = f32[128,128]{1,0:T(8,128)S(1)} custom-call(f32[128,128]{1,0:T(8,128)S(1)} %fusion.54), custom_call_target="Cholesky" | custom-call | tf_op jit(solution)/shard_map/jit(cholesky)/cholesky | solution.py:68
  229.6 9.8 %custom-call.10 = f32[1,128,128]{1,2,0:T(8,128)S(1)} custom-call(f32[1,128,128]{2,1,0:T(8,128)S(1)} %fusion.49), custom_call_target="InvertDiagBlocksLowerTriangular" | custom-call | tf_op jit(solution)/shard_map/jit(_cho_solve)/triangular_solve | solution.py:69
  (62 shorter events, 21.9 us)
Async XLA Ops:
  7.2 207.6 %all-reduce.3.cloned.1.call-start = ((), (), s32[]{:S(2)}) async-start(), calls=%async_computation | async-start | bytes 262144 | tf_op jit(solution)/shard_map/psum | solution.py:64
  15.5 14.2 %copy-start.1 = (f32[1,1,1024]{2,1,0:T(1,128)S(1)}, f32[1,1,1024]{2,1,0:T(1,128)}, u32[]{:S(2)}) copy-start(f32[1,1,1024]{2,1,0:T(1,128)} %param.12) | copy-start | bytes 12292
  15.6 14.2 %copy-start.2 = (f32[1,1,1024]{2,1,0:T(1,128)S(1)}, f32[1,1,1024]{2,1,0:T(1,128)}, u32[]{:S(2)}) copy-start(f32[1,1,1024]{2,1,0:T(1,128)} %param.13) | copy-start | bytes 12292
  15.6 14.2 %copy-start = (bf16[1,1,1024,1024]{3,2,1,0:T(8,128)(2,1)S(1)}, bf16[1,1,1024,1024]{3,2,1,0:T(8,128)(2,1)}, u32[]{:S(2)}) copy-start(bf16[1,1,1024,1024]{3,2,1,0:T(8,128)(2,1)} %param.11) | copy-start | bytes 6291460
  19.2 13.2 %collective-permute-start = (bf16[1,256,128]{2,1,0:T(8,128)(2,1)S(1)}, bf16[1,256,128]{2,1,0:T(8,128)(2,1)S(1)}, u32[]{:S(2)}, u32[]{:S(2)}) collective-permute-start(bf16[1,256,128]{2,1,0:T(8,128)(2,1)S(1)} %get-tuple-element.13), channel_id=1, source_target_pairs={{0,4},{4,8},{8,12},{12,16},{16,20},{20,24},{24,28},{1,5},{5,9},{9,... | collective-permute-start | bytes 196616 | tf_op jit(solution)/shard_map/ppermute | solution.py:12
  24.1 8.3 %collective-permute-start.3 = (bf16[1,256,128]{2,1,0:T(8,128)(2,1)S(1)}, bf16[1,256,128]{2,1,0:T(8,128)(2,1)S(1)}, u32[]{:S(2)}, u32[]{:S(2)}) collective-permute-start(bf16[1,256,128]{2,1,0:T(8,128)(2,1)S(1)} %get-tuple-element.14), channel_id=1, source_target_pairs={{1,0},{2,1},{3,2},{5,4},{6,5},{7,6},{9,8},{10,9},{11,10},{13,12},{... | collective-permute-start | bytes 196616 | tf_op jit(solution)/shard_map/ppermute | solution.py:15
  25.4 7.0 %collective-permute-start.2 = (bf16[1,256,128]{2,1,0:T(8,128)(2,1)S(1)}, bf16[1,256,128]{2,1,0:T(8,128)(2,1)S(1)}, u32[]{:S(2)}, u32[]{:S(2)}) collective-permute-start(bf16[1,256,128]{2,1,0:T(8,128)(2,1)S(1)} %get-tuple-element.15), channel_id=1, source_target_pairs={{0,1},{1,2},{2,3},{4,5},{5,6},{6,7},{8,9},{9,10},{10,11},{12,13},{... | collective-permute-start | bytes 196616 | tf_op jit(solution)/shard_map/ppermute | solution.py:12
  28.4 6.7 %collective-permute-start.1 = (bf16[1,256,128]{2,1,0:T(8,128)(2,1)S(1)}, bf16[1,256,128]{2,1,0:T(8,128)(2,1)S(1)}, u32[]{:S(2)}, u32[]{:S(2)}) collective-permute-start(bf16[1,256,128]{2,1,0:T(8,128)(2,1)S(1)} %get-tuple-element.16), channel_id=1, source_target_pairs={{4,0},{8,4},{12,8},{16,12},{20,16},{24,20},{28,24},{5,1},{9,5},{13... | collective-permute-start | bytes 196616 | tf_op jit(solution)/shard_map/ppermute | solution.py:15
  29.8 2.6 %copy-start.3 = (bf16[1,1,1024]{2,1,0:T(2,128)(2,1)S(1)}, bf16[1,1,1024]{2,1,0:T(2,128)(2,1)}, u32[]{:S(2)}) copy-start(bf16[1,1,1024]{2,1,0:T(2,128)(2,1)} %param.14) | copy-start | bytes 6148
  45.4 10.0 %collective-permute-start.4 = (bf16[1,256,128]{2,1,0:T(8,128)(2,1)S(1)}, bf16[1,256,128]{2,1,0:T(8,128)(2,1)S(1)}, u32[]{:S(2)}, u32[]{:S(2)}) collective-permute-start(bf16[1,256,128]{2,1,0:T(8,128)(2,1)S(1)} %get-tuple-element.9), channel_id=1, source_target_pairs={{0,4},{4,8},{8,12},{12,16},{16,20},{20,24},{24,28},{1,5},{5,9},{9,... | collective-permute-start | bytes 196616 | tf_op jit(solution)/shard_map/ppermute | solution.py:12
  49.8 5.7 %collective-permute-start.7 = (bf16[1,256,128]{2,1,0:T(8,128)(2,1)S(1)}, bf16[1,256,128]{2,1,0:T(8,128)(2,1)S(1)}, u32[]{:S(2)}, u32[]{:S(2)}) collective-permute-start(bf16[1,256,128]{2,1,0:T(8,128)(2,1)S(1)} %get-tuple-element.10), channel_id=1, source_target_pairs={{1,0},{2,1},{3,2},{5,4},{6,5},{7,6},{9,8},{10,9},{11,10},{13,12},{... | collective-permute-start | bytes 196616 | tf_op jit(solution)/shard_map/ppermute | solution.py:15
  51.1 4.4 %collective-permute-start.6 = (bf16[1,256,128]{2,1,0:T(8,128)(2,1)S(1)}, bf16[1,256,128]{2,1,0:T(8,128)(2,1)S(1)}, u32[]{:S(2)}, u32[]{:S(2)}) collective-permute-start(bf16[1,256,128]{2,1,0:T(8,128)(2,1)S(1)} %get-tuple-element.11), channel_id=1, source_target_pairs={{0,1},{1,2},{2,3},{4,5},{5,6},{6,7},{8,9},{9,10},{10,11},{12,13},{... | collective-permute-start | bytes 196616 | tf_op jit(solution)/shard_map/ppermute | solution.py:12
  54.1 6.7 %collective-permute-start.5 = (bf16[1,256,128]{2,1,0:T(8,128)(2,1)S(1)}, bf16[1,256,128]{2,1,0:T(8,128)(2,1)S(1)}, u32[]{:S(2)}, u32[]{:S(2)}) collective-permute-start(bf16[1,256,128]{2,1,0:T(8,128)(2,1)S(1)} %get-tuple-element.12), channel_id=1, source_target_pairs={{4,0},{8,4},{12,8},{16,12},{20,16},{24,20},{28,24},{5,1},{9,5},{13... | collective-permute-start | bytes 196616 | tf_op jit(solution)/shard_map/ppermute | solution.py:15
  72.2 10.8 %collective-permute-start.8 = (bf16[1,256,128]{2,1,0:T(8,128)(2,1)S(1)}, bf16[1,256,128]{2,1,0:T(8,128)(2,1)S(1)}, u32[]{:S(2)}, u32[]{:S(2)}) collective-permute-start(bf16[1,256,128]{2,1,0:T(8,128)(2,1)S(1)} %get-tuple-element.5), channel_id=1, source_target_pairs={{0,4},{4,8},{8,12},{12,16},{16,20},{20,24},{24,28},{1,5},{5,9},{9,... | collective-permute-start | bytes 196616 | tf_op jit(solution)/shard_map/ppermute | solution.py:12
  75.5 7.5 %collective-permute-start.11 = (bf16[1,256,128]{2,1,0:T(8,128)(2,1)S(1)}, bf16[1,256,128]{2,1,0:T(8,128)(2,1)S(1)}, u32[]{:S(2)}, u32[]{:S(2)}) collective-permute-start(bf16[1,256,128]{2,1,0:T(8,128)(2,1)S(1)} %get-tuple-element.6), channel_id=1, source_target_pairs={{1,0},{2,1},{3,2},{5,4},{6,5},{7,6},{9,8},{10,9},{11,10},{13,12},{... | collective-permute-start | bytes 196616 | tf_op jit(solution)/shard_map/ppermute | solution.py:15
  76.8 6.2 %collective-permute-start.10 = (bf16[1,256,128]{2,1,0:T(8,128)(2,1)S(1)}, bf16[1,256,128]{2,1,0:T(8,128)(2,1)S(1)}, u32[]{:S(2)}, u32[]{:S(2)}) collective-permute-start(bf16[1,256,128]{2,1,0:T(8,128)(2,1)S(1)} %get-tuple-element.7), channel_id=1, source_target_pairs={{0,1},{1,2},{2,3},{4,5},{5,6},{6,7},{8,9},{9,10},{10,11},{12,13},{... | collective-permute-start | bytes 196616 | tf_op jit(solution)/shard_map/ppermute | solution.py:12
  79.9 6.8 %collective-permute-start.9 = (bf16[1,256,128]{2,1,0:T(8,128)(2,1)S(1)}, bf16[1,256,128]{2,1,0:T(8,128)(2,1)S(1)}, u32[]{:S(2)}, u32[]{:S(2)}) collective-permute-start(bf16[1,256,128]{2,1,0:T(8,128)(2,1)S(1)} %get-tuple-element.8), channel_id=1, source_target_pairs={{4,0},{8,4},{12,8},{16,12},{20,16},{24,20},{28,24},{5,1},{9,5},{13... | collective-permute-start | bytes 196616 | tf_op jit(solution)/shard_map/ppermute | solution.py:15
Sparse Core Ops, SparseCore 0:
  92.6 122.1 all-reduce.2
where the time goes:
time: 251 us; the launch traced here: 250 us
  waiting for transfers between devices  134 us (53%)
  other arithmetic  41.3 us (16%)
  starting transfers between devices  29.6 us (12%)
  local copies, waits for them, and re-layouts  18.8 us (7%)
  between operations  14.5 us (6%)
  matrix products  12.1 us (5%)
    psum x1, waiting for transfers between devices, gram(): return 0.5 * lax.psum(local_gram(left, right), ('span', 'chord'))  122 us
    ppermute x6, starting transfers between devices, extended(): lax.ppermute(lax.slice_in_dim(block, block.shape[dim] - width, None, axis...  21.6 us
    another operation x3, other arithmetic, spd_solve(): factor = jnp.linalg.cholesky(matrix)  12.4 us
    scatter x3, other arithmetic, exchange_rows(): return jnp.zeros((term.shape[0], width), jnp.float32).at[flat_rows].set(t...  12.2 us
    ppermute x6, waiting for transfers between devices, extended(): lax.ppermute(lax.slice_in_dim(block, 0, width, axis=dim), axis, backward)  11.8 us
    another operation x2, other arithmetic, spd_solve(): return jax.scipy.linalg.cho_solve((factor, True), rhs)  10.5 us
    gather x3, local copies, waits for them, and re-layouts, exchange_rows(): sent = jnp.take(term, flat_rows, axis=0).reshape(4, slots, width)  9.63 us
    ppermute x6, starting transfers between devices, extended(): lax.ppermute(lax.slice_in_dim(block, 0, width, axis=dim), axis, backward)  7.93 us
  transfers between devices with their start and end apart: 13, of which 4 were waited for; matrix products, arithmetic and copies ran while one was open for 2% of the time, Pallas kernels for 0%

commit v1 on v0

v1 whole, which is shorter than its diff:
```python
import functools

import jax
import jax.numpy as jnp
from jax import lax
from jax.experimental import pallas as pl
from jax.experimental.pallas import tpu as pltpu
from jax.sharding import PartitionSpec as P

MESH = pl.DeviceIdType.MESH
SIDES = (("span", -1), ("span", 1), ("chord", -1), ("chord", 1))
NT = (((1,), (1,)), ((), ()))


def digits(count):
    out, stride = [], 1
    while count > 1:
        if count % 4 == 0 and out:
            radix = 4
        else:
            radix = next(f for f in range(2, count + 1) if count % f == 0)
        out.append((radix, stride))
        stride *= radix
        count //= radix
    return out


def dot(a, b):
    return jnp.dot(a, b, preferred_element_type=jnp.float32)


def dot_nt(a, b):
    return lax.dot_general(a, b, NT, preferred_element_type=jnp.float32)


def fields_kernel(
    spans,
    chords,
    disp_ref,
    packed_ref,
    fscale_ref,
    dscale_ref,
    diag_ref,
    rows_ref,
    signs_ref,
    counts_ref,
    precond_ref,
    image_ref,
    residual_ref,
    gamma_ref,
    curv_ref,
    hot,
    fdiag,
    ddiag,
    sent,
    recv,
    acc,
    scattered,
    held,
    fan,
    full,
    side_send,
    side_recv,
    red_send,
    red_recv,
):
    size, loads = disp_ref.shape[2:]
    slots = rows_ref.shape[3]
    tile = fdiag.shape[1]
    tiles = size // tile
    pos = {"span": lax.axis_index("span"), "chord": lax.axis_index("chord")}
    limit = {"span": spans, "chord": chords}
    steps = digits(spans)
    chunk = loads // chords

    def chord_peer(k):
        return lax.rem(pos["chord"] + k, chords)

    def span_peer(radix, stride, k):
        digit = lax.rem(pos["span"] // stride, radix)
        return pos["span"] + (lax.rem(digit + k, radix) - digit) * stride

    barrier = pltpu.get_barrier_semaphore()
    greeted = [{"chord": chord_peer(k)} for k in range(1, chords)]
    greeted += [{"span": lax.rem(pos["span"] + k, spans)} for k in (1, spans - 1)]
    greeted += [
        {"span": span_peer(radix, stride, k)} for radix, stride in steps for k in range(1, radix)
    ]
    for device in greeted:
        pl.semaphore_signal(barrier, inc=1, device_id=device, device_id_type=MESH)

    live_signs = []
    for d in range(4):
        rows = rows_ref[0, 0, d : d + 1, :]
        row_ids = lax.broadcasted_iota(jnp.int32, (size, slots), 0)
        hot[:, d * slots : (d + 1) * slots] = jnp.where(row_ids == rows, 1.0, 0.0).astype(
            jnp.bfloat16
        )
        live = lax.broadcasted_iota(jnp.int32, (1, slots), 1) < counts_ref[0, 0, d]
        live_signs.append(
            jnp.where(live, signs_ref[0, 0, d : d + 1, :], 0).astype(jnp.float32)
        )
    signs = jnp.concatenate(live_signs, axis=1)
    signs = jnp.broadcast_to(signs, (16, size)).astype(jnp.bfloat16)
    sign = dot_nt(signs, hot[...])[0:1, :]

    def neighbour(d):
        axis, step = SIDES[d]
        other = pos[axis] + step
        return jnp.logical_and(other >= 0, other < limit[axis])

    def side_copy(e, d, slot):
        axis, step = SIDES[d]
        return pltpu.make_async_remote_copy(
            src_ref=sent.at[e, d],
            dst_ref=recv.at[e, slot],
            send_sem=side_send.at[e, d],
            recv_sem=side_recv.at[e, slot],
            device_id={axis: pos[axis] + step},
            device_id_type=MESH,
        )

    def send(e, term):
        values = dot(term, hot[...]).astype(jnp.bfloat16)
        for d in range(4):
            sent[e, d] = values[:, d * slots : (d + 1) * slots]
        for d in range(4):

            @pl.when(neighbour(d))
            def _():
                side_copy(e, d, d ^ 1).start()

    def partner(e):
        for d in range(4):

            @pl.when(neighbour(d))
            def _():
                side_copy(e, d, d).wait_recv()

        values = jnp.concatenate([recv[e, d] for d in range(4)], axis=1)
        return dot_nt(values, hot[...]).astype(jnp.bfloat16)

    def apply(diag_blocks, upper, scale, field):
        operand = (scale * sign * field).astype(jnp.bfloat16)
        out = []
        for b in range(tiles):
            lo, hi = b * tile, (b + 1) * tile
            total = dot(operand[:, lo:hi], diag_blocks[b])
            if upper:
                direct, mirrored = (0, lo), (hi, size)
            else:
                direct, mirrored = (hi, size), (0, lo)
            if direct[0] < direct[1]:
                total += dot(
                    operand[:, direct[0] : direct[1]],
                    packed_ref[0, 0, direct[0] : direct[1], lo:hi],
                )
            if mirrored[0] < mirrored[1]:
                total += dot_nt(
                    operand[:, mirrored[0] : mirrored[1]],
                    packed_ref[0, 0, lo:hi, mirrored[0] : mirrored[1]],
                )
            out.append(total)
        product = jnp.concatenate(out, axis=1)
        return (sign * scale * product).astype(jnp.bfloat16)

    def pair_gram(left, right):
        return sum(dot_nt(a, b) for a in left for b in right)

    def total_of(pair):
        return pair[0].astype(jnp.float32) + pair[1].astype(jnp.float32)

    class Reduction:
        def __init__(self, g):
            self.g, self.stage = g, 0

        def copy(self, n, src, dst, device):
            return pltpu.make_async_remote_copy(
                src_ref=src,
                dst_ref=dst,
                send_sem=red_send.at[self.g, n],
                recv_sem=red_recv.at[self.g, n],
                device_id=device,
                device_id_type=MESH,
            )

        def copies(self, stage):
            g, me = self.g, pos["chord"]
            if stage == 0:
                return [
                    self.copy(
                        k - 1,
                        acc.at[g, pl.ds(pl.multiple_of(chord_peer(k) * chunk, chunk), chunk)],
                        scattered.at[g, k - 1],
                        {"chord": chord_peer(k)},
                    )
                    for k in range(1, chords)
                ]
            first = chords - 1
            fans = [radix - 1 for radix, _ in steps]
            if stage <= len(steps):
                radix, stride = steps[stage - 1]
                base = sum(fans[: stage - 1])
                return [
                    self.copy(
                        first + base + k - 1,
                        held.at[g, stage - 1],
                        fan.at[g, base + k - 1],
                        {"span": span_peer(radix, stride, k)},
                    )
                    for k in range(1, radix)
                ]
            first += sum(fans)
            mine = pl.ds(pl.multiple_of(me * chunk, chunk), chunk)
            return [
                self.copy(
                    first + k - 1,
                    held.at[g, len(steps)],
                    full.at[g, mine],
                    {"chord": chord_peer(k)},
                )
                for k in range(1, chords)
            ]

        def start(self, value):
            acc[self.g] = value
            for copy in self.copies(0):
                copy.start()

        def advance(self):
            if self.stage > len(steps) + 1:
                return
            g, stage = self.g, self.stage
            copies = self.copies(stage)
            for copy in copies:
                copy.wait_recv()
            mine = pl.ds(pl.multiple_of(pos["chord"] * chunk, chunk), chunk)
            if stage == 0:
                total = acc[g, mine]
                for k in range(1, chords):
                    total += scattered[g, k - 1]
            elif stage <= len(steps):
                base = sum(radix - 1 for radix, _ in steps[: stage - 1])
                total = held[g, stage - 1]
                for k in range(steps[stage - 1][0] - 1):
                    total += fan[g, base + k]
            if stage <= len(steps):
                held[g, stage] = total
                if stage == len(steps):
                    full[g, mine] = total
                for copy in self.copies(stage + 1):
                    copy.start()
            self.stage += 1

        def finish(self):
            while self.stage <= len(steps) + 1:
                self.advance()
            for stage in range(len(steps) + 2):
                for copy in self.copies(stage):
                    copy.wait_send()

    disp = disp_ref[0, 0].astype(jnp.float32).T
    gap = (sign * disp).astype(jnp.bfloat16)
    for d in range(4):

        @pl.when(jnp.logical_not(neighbour(d)))
        def _():
            for e in range(3):
                recv[e, d] = jnp.zeros(recv.shape[2:], recv.dtype)

    pl.semaphore_wait(barrier, len(greeted))
    send(0, gap)
    for b in range(tiles):
        lo, hi = b * tile, (b + 1) * tile
        here = packed_ref[0, 0, lo:hi, lo:hi].astype(jnp.float32)
        mirror = here.T
        row_ids = lax.broadcasted_iota(jnp.int32, (tile, tile), 0)
        col_ids = lax.broadcasted_iota(jnp.int32, (tile, tile), 1)
        fdiag[b] = jnp.where(col_ids >= row_ids, here, mirror).astype(jnp.bfloat16)
        lower = jnp.where(row_ids > col_ids, here, mirror)
        diag = diag_ref[0, :, lo:hi].astype(jnp.float32)
        ddiag[b] = jnp.where(row_ids == col_ids, diag, lower).astype(jnp.bfloat16)
    fscale = fscale_ref[0]
    dscale = dscale_ref[0]

    right = (gap, partner(0))
    residual = total_of(right)
    term = apply(ddiag, False, dscale, residual)
    send(1, term)
    residual_ref[...] = residual.T
    precond = (term, partner(1))
    direction = total_of(precond)
    gamma = Reduction(0)
    gamma.start(pair_gram(precond, right))
    term = apply(fdiag, True, fscale, direction)
    send(2, term)
    gamma.advance()
    precond_ref[...] = direction.T
    image = (term, partner(2))
    curv = Reduction(1)
    curv.start(pair_gram(precond, image))
    gamma.advance()
    image_ref[...] = total_of(image).T
    curv.advance()
    gamma.advance()
    curv.advance()
    gamma.advance()
    curv.finish()
    gamma.finish()
    gamma_ref[...] = full[0]
    curv_ref[...] = full[1]
    for e in range(3):
        for d in range(4):

            @pl.when(neighbour(d))
            def _():
                side_copy(e, d, d).wait_send()


def update_kernel(precond_ref, image_ref, residual_ref, gamma_ref, curv_ref, mult_ref, res_ref):
    loads = curv_ref.shape[0]
    width = 8
    matrix = curv_ref[...]
    matrix = 0.5 * (matrix + matrix.T)
    rhs = gamma_ref[...]
    count = loads // width
    left = [matrix[p * width : (p + 1) * width] for p in range(count)]
    right = [rhs[p * width : (p + 1) * width] for p in range(count)]
    shape = (width, loads)
    sub_ids = lax.broadcasted_iota(jnp.int32, shape, 0)

    def column(block, c):
        return jnp.broadcast_to(block[:, c : c + 1], shape)

    def row(block, r):
        return jnp.broadcast_to(block[r : r + 1, :], shape)

    for p in range(count):
        here, there = left[p], right[p]
        cols = [column(here, p * width + j) for j in range(width)]
        for j in range(width):
            inverse = 1.0 / row(cols[j], j)

            def eliminate(block):
                pivot = row(block, j) * inverse
                return jnp.where(sub_ids == j, pivot, block - cols[j] * pivot)

            here, there = eliminate(here), eliminate(there)
            cols = cols[: j + 1] + [eliminate(c) for c in cols[j + 1 :]]
        left[p], right[p] = here, there
        rows_left = [row(here, j) for j in range(width)]
        rows_right = [row(there, j) for j in range(width)]
        order = [(p + k) % count for k in range(1, count)]
        for r in order:
            factors = [column(left[r], p * width + j) for j in range(width)]
            for j in range(width):
                right[r] = right[r] - factors[j] * rows_right[j]
            if p + 1 < count:
                for j in range(width):
                    left[r] = left[r] - factors[j] * rows_left[j]
    alpha = jnp.concatenate(right, axis=0)

    def mat_right(field):
        return jnp.dot(
            field, alpha, precision=lax.Precision.HIGHEST, preferred_element_type=jnp.float32
        )

    mult_ref[0, 0] = mat_right(precond_ref[...])
    res_ref[0, 0] = residual_ref[...] - mat_right(image_ref[...])


def shards(spans, chords, *args):
    displacement, packed, link_rows = args[0], args[1], args[5]
    size, loads = displacement.shape[2:]
    slots = link_rows.shape[3]
    tile = min(256, size)
    steps = digits(spans)
    fans = sum(radix - 1 for radix, _ in steps)
    sems = 2 * (chords - 1) + fans
    chunk = loads // chords
    f32, bf16 = jnp.float32, jnp.bfloat16
    vmem = pl.BlockSpec(memory_space=pltpu.VMEM)
    smem = pl.BlockSpec(memory_space=pltpu.SMEM)
    field = jax.ShapeDtypeStruct((size, loads), f32)
    small = jax.ShapeDtypeStruct((loads, loads), f32)
    middle = pl.pallas_call(
        functools.partial(fields_kernel, spans, chords),
        out_shape=(field, field, field, small, small),
        in_specs=[vmem] * 7 + [smem],
        out_specs=(vmem,) * 5,
        scratch_shapes=[
            pltpu.VMEM((size, size), bf16),
            pltpu.VMEM((size // tile, tile, tile), bf16),
            pltpu.VMEM((size // tile, tile, tile), bf16),
            pltpu.VMEM((3, 4, loads, slots), bf16),
            pltpu.VMEM((3, 4, loads, slots), bf16),
            pltpu.VMEM((2, loads, loads), f32),
            pltpu.VMEM((2, chords - 1, chunk, loads), f32),
            pltpu.VMEM((2, len(steps) + 1, chunk, loads), f32),
            pltpu.VMEM((2, fans, chunk, loads), f32),
            pltpu.VMEM((2, loads, loads), f32),
            pltpu.SemaphoreType.DMA((3, 4)),
            pltpu.SemaphoreType.DMA((3, 4)),
            pltpu.SemaphoreType.DMA((2, sems)),
            pltpu.SemaphoreType.DMA((2, sems)),
        ],
        compiler_params=pltpu.CompilerParams(
            collective_id=0, has_side_effects=True, vmem_limit_bytes=40 * 1024 * 1024
        ),
        name="fields",
    )(*args)
    out = jax.ShapeDtypeStruct((1, 1, size, loads), f32)
    return pl.pallas_call(
        update_kernel,
        out_shape=(out, out),
        in_specs=[vmem] * 5,
        out_specs=(vmem, vmem),
        compiler_params=pltpu.CompilerParams(vmem_limit_bytes=40 * 1024 * 1024),
        name="update",
    )(*middle)


def solution(mesh):
    wide = P("span", "chord", None, None)
    narrow = P("span", "chord", None)
    return jax.shard_map(
        functools.partial(shards, mesh.shape["span"], mesh.shape["chord"]),
        mesh=mesh,
        in_specs=(wide, wide, narrow, narrow, narrow, wide, wide, narrow),
        out_specs=(wide, wide),
        check_vma=False,
    )
```

time: 251 us -> 50.5 us (0.20)
  waiting for transfers between devices: 134 us -> 0 us
  Pallas kernels: 0 us -> 42.9 us
  other arithmetic: 41.3 us -> 0 us
  starting transfers between devices: 29.6 us -> 0 us
  between operations: 14.5 us -> 0.66 us
  local copies, waits for them, and re-layouts: 18.8 us -> 6.62 us
  matrix products: 12.1 us -> 0 us
    psum x1 -> x0, waiting for transfers between devices: 122 us -> none  [gram(): return 0.5 * lax.psum(local_gram(left, right), ('span', 'chord'))]
    pallas_call x0 -> x2, Pallas kernels: none -> 42.9 us  [the longest x1 36.6 us: shards(): pl.pallas_call(functools.partial(fields_kernel, spans, chords), out_shape...]
    ppermute x12 -> x0, starting transfers between devices: 29.5 us -> none  [the longest x6 21.6 us: extended(): lax.ppermute(lax.slice_in_dim(block, block.shape[dim] - width, None, axis...]
    another operation x8 -> x0, other arithmetic: 23 us -> none  [the longest x3 12.4 us: spd_solve(): factor = jnp.linalg.cholesky(matrix)]
    scatter x3 -> x0, other arithmetic: 12.2 us -> none  [exchange_rows(): return jnp.zeros((term.shape[0], width), jnp.float32).at[flat_rows].set(t...]
    ppermute x12 -> x0, waiting for transfers between devices: 11.8 us -> none  [the longest x6 11.8 us: extended(): lax.ppermute(lax.slice_in_dim(block, 0, width, axis=dim), axis, backward)]
    dot_general x6 -> x0, matrix products: 10.8 us -> none  [the longest x2 4.82 us: local_term(): product = jnp.dot(block, operand, preferred_element_type=jnp.float32)]
    gather x3 -> x0, local copies, waits for them, and re-layouts: 9.63 us -> none  [exchange_rows(): sent = jnp.take(term, flat_rows, axis=0).reshape(4, slots, width)]
  transfers between devices with their start and end apart: 13 -> 0, of which waited for: 4 -> 0; matrix products, arithmetic and copies ran while one was open for 2% -> 0% of each run, Pallas kernels for 0% -> 0%
where the time goes in v1:
time: 50.5 us; the launch traced here: 50.2 us
  Pallas kernels  42.9 us (85%)
  local copies, waits for them, and re-layouts  6.62 us (13%)
  between operations  0.66 us (1%)
    pallas_call x1, Pallas kernels, shards(): pl.pallas_call(functools.partial(fields_kernel, spans, chords), out_shape...  36.6 us
    unnamed x16, local copies, waits for them, and re-layouts  6.62 us
    pallas_call x1, Pallas kernels, shards(): pl.pallas_call(update_kernel, out_shape=(out, out), in_specs=[vmem] * 5,...  6.28 us

profile of v1, /device:TPU:0, one launch (start us, length us, event | category | flops | bytes accessed | tf_op | source)
XLA Modules:
  0.0 50.2 jit_solution(4691102945503102486)
XLA Ops:
  0.6 0.0 copy-start
  0.6 1.6 %copy-done = bf16[1,1,1024,1024]{3,2,1,0:T(8,128)(2,1)S(1)} copy-done((bf16[1,1,1024,1024]{3,2,1,0:T(8,128)(2,1)S(1)}, bf16[1,1,1024,1024]{3,2,1,0:T(8,128)(2,1)}, u32[]{:S(2)}) %copy-start) | copy-done | bytes 2097176
  2.2 0.0 copy-start.1
  2.2 0.9 %copy-done.1 = bf16[1,1,1024,128]{3,2,1,0:T(8,128)(2,1)S(1)} copy-done((bf16[1,1,1024,128]{3,2,1,0:T(8,128)(2,1)S(1)}, bf16[1,1,1024,128]{3,2,1,0:T(8,128)(2,1)}, u32[]{:S(2)}) %copy-start.1) | copy-done | bytes 262168
  3.2 0.0 copy-start.2
  3.2 0.7 %copy-done.2 = f32[1,1,1024]{2,1,0:T(1,128)S(1)} copy-done((f32[1,1,1024]{2,1,0:T(1,128)S(1)}, f32[1,1,1024]{2,1,0:T(1,128)}, u32[]{:S(2)}) %copy-start.2) | copy-done | bytes 4120
  3.9 0.0 copy-start.3
  3.9 0.7 %copy-done.3 = f32[1,1,1024]{2,1,0:T(1,128)S(1)} copy-done((f32[1,1,1024]{2,1,0:T(1,128)S(1)}, f32[1,1,1024]{2,1,0:T(1,128)}, u32[]{:S(2)}) %copy-start.3) | copy-done | bytes 4120
  4.5 0.0 copy-start.4
  4.6 0.7 %copy-done.4 = bf16[1,1,1024]{2,1,0:T(2,128)(2,1)S(1)} copy-done((bf16[1,1,1024]{2,1,0:T(2,128)(2,1)S(1)}, bf16[1,1,1024]{2,1,0:T(2,128)(2,1)}, u32[]{:S(2)}) %copy-start.4) | copy-done | bytes 2072
  5.2 0.0 copy-start.5
  5.2 0.7 %copy-done.5 = s32[1,1,4,256]{3,2,1,0:T(4,128)S(1)} copy-done((s32[1,1,4,256]{3,2,1,0:T(4,128)S(1)}, s32[1,1,4,256]{3,2,1,0:T(4,128)}, u32[]{:S(2)}) %copy-start.5) | copy-done | bytes 4120
  5.9 0.0 copy-start.6
  5.9 0.7 %copy-done.6 = s32[1,1,4,256]{3,2,1,0:T(4,128)S(1)} copy-done((s32[1,1,4,256]{3,2,1,0:T(4,128)S(1)}, s32[1,1,4,256]{3,2,1,0:T(4,128)}, u32[]{:S(2)}) %copy-start.6) | copy-done | bytes 4120
  6.6 0.0 copy-start.7
  6.6 0.7 %copy-done.7 = s32[1,1,4]{2,1,0:T(1,128)S(1)} copy-done((s32[1,1,4]{2,1,0:T(1,128)S(1)}, s32[1,1,4]{2,1,0:T(1,128)}, u32[]{:S(2)}) %copy-start.7) | copy-done | bytes 40
  7.3 36.6 %fields.1 = (f32[1024,128]{1,0:T(8,128)S(1)}, f32[1024,128]{1,0:T(8,128)S(1)}, f32[1024,128]{1,0:T(8,128)S(1)}, f32[128,128]{1,0:T(8,128)S(1)}, f32[128,128]{1,0:T(8,128)S(1)}) custom-call(bf16[1,1,1024,128]{3,2,1,0:T(8,128)(2,1)S(1)} %copy-done.1, bf16[1,1,1024,1024]{3,2,1,0:T(8,128)(2,1)S(1)} %copy-done, f32[1,1,1024]{2,1,0:T(1,128)S(1)} %copy-done.2, ...), custom_call_target="tpu_custom_call" | custom-call | tf_op jit(solution)/shard_map/fields/pallas_call | solution.py:386
  43.9 6.3 %update.1 = (f32[1,1,1024,128]{3,2,1,0:T(8,128)}, f32[1,1,1024,128]{3,2,1,0:T(8,128)}) custom-call(f32[1024,128]{1,0:T(8,128)S(1)} %get-tuple-element.7.precond_ref, f32[1024,128]{1,0:T(8,128)S(1)} %get-tuple-element.8.image_ref, f32[1024,128]{1,0:T(8,128)S(1)} %get-tuple-element.9.residual_ref, f32[128,128]{1,0:T(8,128)S(1)} %get-tuple-element.10.gamma_ref, ...), custom_call_target="tpu_custom_call" | custom-call | tf_op jit(solution)/shard_map/update/pallas_call | solution.py:413
Async XLA Ops:
  0.6 1.6 %copy-start = (bf16[1,1,1024,1024]{3,2,1,0:T(8,128)(2,1)S(1)}, bf16[1,1,1024,1024]{3,2,1,0:T(8,128)(2,1)}, u32[]{:S(2)}) copy-start(bf16[1,1,1024,1024]{3,2,1,0:T(8,128)(2,1)} %packed_ref.1) | copy-start | bytes 6291460
  2.2 0.9 %copy-start.1 = (bf16[1,1,1024,128]{3,2,1,0:T(8,128)(2,1)S(1)}, bf16[1,1,1024,128]{3,2,1,0:T(8,128)(2,1)}, u32[]{:S(2)}) copy-start(bf16[1,1,1024,128]{3,2,1,0:T(8,128)(2,1)} %disp_ref.1) | copy-start | bytes 786436
  3.2 0.7 %copy-start.2 = (f32[1,1,1024]{2,1,0:T(1,128)S(1)}, f32[1,1,1024]{2,1,0:T(1,128)}, u32[]{:S(2)}) copy-start(f32[1,1,1024]{2,1,0:T(1,128)} %fscale_ref.1) | copy-start | bytes 12292
  3.9 0.7 %copy-start.3 = (f32[1,1,1024]{2,1,0:T(1,128)S(1)}, f32[1,1,1024]{2,1,0:T(1,128)}, u32[]{:S(2)}) copy-start(f32[1,1,1024]{2,1,0:T(1,128)} %dscale_ref.1) | copy-start | bytes 12292
  4.5 0.7 %copy-start.4 = (bf16[1,1,1024]{2,1,0:T(2,128)(2,1)S(1)}, bf16[1,1,1024]{2,1,0:T(2,128)(2,1)}, u32[]{:S(2)}) copy-start(bf16[1,1,1024]{2,1,0:T(2,128)(2,1)} %diag_ref.1) | copy-start | bytes 6148
  5.2 0.7 %copy-start.5 = (s32[1,1,4,256]{3,2,1,0:T(4,128)S(1)}, s32[1,1,4,256]{3,2,1,0:T(4,128)}, u32[]{:S(2)}) copy-start(s32[1,1,4,256]{3,2,1,0:T(4,128)} %rows_ref.1) | copy-start | bytes 12292
  5.9 0.7 %copy-start.6 = (s32[1,1,4,256]{3,2,1,0:T(4,128)S(1)}, s32[1,1,4,256]{3,2,1,0:T(4,128)}, u32[]{:S(2)}) copy-start(s32[1,1,4,256]{3,2,1,0:T(4,128)} %signs_ref.1) | copy-start | bytes 12292
  6.6 0.7 %copy-start.7 = (s32[1,1,4]{2,1,0:T(1,128)S(1)}, s32[1,1,4]{2,1,0:T(1,128)}, u32[]{:S(2)}) copy-start(s32[1,1,4]{2,1,0:T(1,128)} %counts_ref.1) | copy-start | bytes 52

commit v2 on v1

--- a/solution.py
+++ b/solution.py
@@ -36,19 +36,13 @@
 def fields_kernel(
     spans,
     chords,
-    disp_ref,
-    packed_ref,
-    fscale_ref,
-    dscale_ref,
-    diag_ref,
-    rows_ref,
-    signs_ref,
-    counts_ref,
-    precond_ref,
-    image_ref,
-    residual_ref,
-    gamma_ref,
-    curv_ref,
+    *refs,
+):
+    inputs, refs = refs[:8], refs[8:]
+    outputs = refs[:5]
+    local, refs = refs[5:13], refs[13:]
+    disp_ref, packed_ref, fscale_ref, dscale_ref, diag_ref, rows_ref, signs_ref, counts_ref = local
+    (
     hot,
     fdiag,
     ddiag,
@@ -63,25 +57,43 @@
     side_recv,
     red_send,
     red_recv,
-):
+    load_sem,
+    precond_ref,
+    image_ref,
+    residual_ref,
+    store_sem,
+    ) = refs
     size, loads = disp_ref.shape[2:]
     slots = rows_ref.shape[3]
     tile = fdiag.shape[1]
     tiles = size // tile
     pos = {"span": lax.axis_index("span"), "chord": lax.axis_index("chord")}
     limit = {"span": spans, "chord": chords}
-    steps = digits(spans)
-    chunk = loads // chords
-
-    def chord_peer(k):
-        return lax.rem(pos["chord"] + k, chords)
+    (near, _), *steps = digits(spans)
+    group = chords * near
+    chunk = loads // group
+
+    loading = [
+        pltpu.make_async_copy(inputs[n], local[n], load_sem.at[n]) for n in range(8)
+    ]
+    for n in (5, 0, 6, 7, 1, 3, 4, 2):
+        loading[n].start()
 
     def span_peer(radix, stride, k):
         digit = lax.rem(pos["span"] // stride, radix)
         return pos["span"] + (lax.rem(digit + k, radix) - digit) * stride
 
+    def group_peer(m):
+        chord = lax.rem(pos["chord"] + m // near, chords)
+        device = {"span": span_peer(near, 1, m % near), "chord": chord}
+        return device, chord * near + lax.rem(device["span"], near)
+
+    mine = pl.ds(
+        pl.multiple_of((pos["chord"] * near + lax.rem(pos["span"], near)) * chunk, chunk), chunk
+    )
+
     barrier = pltpu.get_barrier_semaphore()
-    greeted = [{"chord": chord_peer(k)} for k in range(1, chords)]
+    greeted = [group_peer(m)[0] for m in range(1, group)]
     greeted += [{"span": lax.rem(pos["span"] + k, spans)} for k in (1, spans - 1)]
     greeted += [
         {"span": span_peer(radix, stride, k)} for radix, stride in steps for k in range(1, radix)
@@ -89,6 +101,8 @@
     for device in greeted:
         pl.semaphore_signal(barrier, inc=1, device_id=device, device_id_type=MESH)
 
+    for n in (5, 6, 7):
+        loading[n].wait()
     live_signs = []
     for d in range(4):
         rows = rows_ref[0, 0, d : d + 1, :]
@@ -96,13 +110,11 @@
         hot[:, d * slots : (d + 1) * slots] = jnp.where(row_ids == rows, 1.0, 0.0).astype(
             jnp.bfloat16
         )
-        live = lax.broadcasted_iota(jnp.int32, (1, slots), 1) < counts_ref[0, 0, d]
+        live = lax.broadcasted_iota(jnp.int32, (1, slots), 1) < counts_ref[0, :, d : d + 1]
         live_signs.append(
             jnp.where(live, signs_ref[0, 0, d : d + 1, :], 0).astype(jnp.float32)
         )
-    signs = jnp.concatenate(live_signs, axis=1)
-    signs = jnp.broadcast_to(signs, (16, size)).astype(jnp.bfloat16)
-    sign = dot_nt(signs, hot[...])[0:1, :]
+    slot_sign = jnp.concatenate(live_signs, axis=1)
 
     def neighbour(d):
         axis, step = SIDES[d]
@@ -120,25 +132,32 @@
             device_id_type=MESH,
         )
 
-    def send(e, term):
-        values = dot(term, hot[...]).astype(jnp.bfloat16)
-        for d in range(4):
-            sent[e, d] = values[:, d * slots : (d + 1) * slots]
-        for d in range(4):
-
-            @pl.when(neighbour(d))
-            def _():
-                side_copy(e, d, d ^ 1).start()
+    def send(e, term, scale=None):
+        for pair in ((0, 1), (2, 3)):
+            here = slice(pair[0] * slots, (pair[1] + 1) * slots)
+            values = dot(term, hot[:, here])
+            if scale is not None:
+                values = values * scale[:, here]
+            values = values.astype(jnp.bfloat16)
+            for d in pair:
+                sent[e, d] = values[:, (d - pair[0]) * slots : (d - pair[0] + 1) * slots]
+
+                @pl.when(neighbour(d))
+                def _():
+                    side_copy(e, d, d ^ 1).start()
 
     def partner(e):
-        for d in range(4):
-
-            @pl.when(neighbour(d))
-            def _():
-                side_copy(e, d, d).wait_recv()
-
-        values = jnp.concatenate([recv[e, d] for d in range(4)], axis=1)
-        return dot_nt(values, hot[...]).astype(jnp.bfloat16)
+        total = 0
+        for pair in ((2, 3), (0, 1)):
+            for d in pair:
+
+                @pl.when(neighbour(d))
+                def _():
+                    side_copy(e, d, d).wait_recv()
+
+            values = jnp.concatenate([recv[e, d] for d in pair], axis=1)
+            total += dot_nt(values, hot[:, pair[0] * slots : (pair[1] + 1) * slots])
+        return total.astype(jnp.bfloat16)
 
     def apply(diag_blocks, upper, scale, field):
         operand = (scale * sign * field).astype(jnp.bfloat16)
@@ -185,18 +204,15 @@
             )
 
         def copies(self, stage):
-            g, me = self.g, pos["chord"]
+            g = self.g
             if stage == 0:
-                return [
-                    self.copy(
-                        k - 1,
-                        acc.at[g, pl.ds(pl.multiple_of(chord_peer(k) * chunk, chunk), chunk)],
-                        scattered.at[g, k - 1],
-                        {"chord": chord_peer(k)},
-                    )
-                    for k in range(1, chords)
-                ]
-            first = chords - 1
+                out = []
+                for m in range(1, group):
+                    device, owner = group_peer(m)
+                    rows = pl.ds(pl.multiple_of(owner * chunk, chunk), chunk)
+                    out.append(self.copy(m - 1, acc.at[g, rows], scattered.at[g, m - 1], device))
+                return out
+            first = group - 1
             fans = [radix - 1 for radix, _ in steps]
             if stage <= len(steps):
                 radix, stride = steps[stage - 1]
@@ -211,15 +227,11 @@
                     for k in range(1, radix)
                 ]
             first += sum(fans)
-            mine = pl.ds(pl.multiple_of(me * chunk, chunk), chunk)
             return [
                 self.copy(
-                    first + k - 1,
-                    held.at[g, len(steps)],
-                    full.at[g, mine],
-                    {"chord": chord_peer(k)},
+                    first + m - 1, held.at[g, len(steps)], full.at[g, mine], group_peer(m)[0]
                 )
-                for k in range(1, chords)
+                for m in range(1, group)
             ]
 
         def start(self, value):
@@ -234,11 +246,10 @@
             copies = self.copies(stage)
             for copy in copies:
                 copy.wait_recv()
-            mine = pl.ds(pl.multiple_of(pos["chord"] * chunk, chunk), chunk)
             if stage == 0:
                 total = acc[g, mine]
-                for k in range(1, chords):
-                    total += scattered[g, k - 1]
+                for m in range(1, group):
+                    total += scattered[g, m - 1]
             elif stage <= len(steps):
                 base = sum(radix - 1 for radix, _ in steps[: stage - 1])
                 total = held[g, stage - 1]
@@ -259,8 +270,17 @@
                 for copy in self.copies(stage):
                     copy.wait_send()
 
+    def lay(ref, pair):
+        for n, part in enumerate(pair):
+            ref[:, n * loads : (n + 1) * loads] = part.astype(jnp.float32).T.astype(ref.dtype)
+
+    stored = (precond_ref, image_ref, residual_ref, full.at[0], full.at[1])
+    storing = [
+        pltpu.make_async_copy(stored[n], outputs[n], store_sem.at[n]) for n in range(5)
+    ]
+
+    loading[0].wait()
     disp = disp_ref[0, 0].astype(jnp.float32).T
-    gap = (sign * disp).astype(jnp.bfloat16)
     for d in range(4):
 
         @pl.when(jnp.logical_not(neighbour(d)))
@@ -269,7 +289,12 @@
                 recv[e, d] = jnp.zeros(recv.shape[2:], recv.dtype)
 
     pl.semaphore_wait(barrier, len(greeted))
-    send(0, gap)
+    send(0, disp.astype(jnp.bfloat16), slot_sign)
+    signs = jnp.broadcast_to(slot_sign, (16, size)).astype(jnp.bfloat16)
+    sign = dot_nt(signs, hot[...])[0:1, :]
+    gap = (sign * disp).astype(jnp.bfloat16)
+    for n in (1, 2, 3, 4):
+        loading[n].wait()
     for b in range(tiles):
         lo, hi = b * tile, (b + 1) * tile
         here = packed_ref[0, 0, lo:hi, lo:hi].astype(jnp.float32)
@@ -288,6 +313,7 @@
     term = apply(ddiag, False, dscale, residual)
     send(1, term)
     residual_ref[...] = residual.T
+    storing[2].start()
     precond = (term, partner(1))
     direction = total_of(precond)
     gamma = Reduction(0)
@@ -295,20 +321,23 @@
     term = apply(fdiag, True, fscale, direction)
     send(2, term)
     gamma.advance()
-    precond_ref[...] = direction.T
+    lay(precond_ref, precond)
+    storing[0].start()
+    early = pair_gram(precond, (term,))
     image = (term, partner(2))
     curv = Reduction(1)
-    curv.start(pair_gram(precond, image))
+    curv.start(early + pair_gram(precond, image[1:]))
     gamma.advance()
-    image_ref[...] = total_of(image).T
+    lay(image_ref, image)
+    storing[1].start()
     curv.advance()
     gamma.advance()
     curv.advance()
     gamma.advance()
+    gamma.finish()
+    storing[3].start()
     curv.finish()
-    gamma.finish()
-    gamma_ref[...] = full[0]
-    curv_ref[...] = full[1]
+    storing[4].start()
     for e in range(3):
         for d in range(4):
 
@@ -316,8 +345,24 @@
             def _():
                 side_copy(e, d, d).wait_send()
 
-
-def update_kernel(precond_ref, image_ref, residual_ref, gamma_ref, curv_ref, mult_ref, res_ref):
+    for copy in storing:
+        copy.wait()
+
+
+def update_kernel(*refs):
+    inputs, outputs, local = refs[:5], refs[5:7], refs[7:14]
+    load_sem, store_sem = refs[14:]
+    precond_ref, image_ref, residual_ref, gamma_ref, curv_ref, mult_ref, res_ref = local
+    loading = [
+        pltpu.make_async_copy(inputs[n], local[n], load_sem.at[n]) for n in range(5)
+    ]
+    storing = [
+        pltpu.make_async_copy(local[5 + n], outputs[n].at[0, 0], store_sem.at[n]) for n in range(2)
+    ]
+    for copy in loading[::-1]:
+        copy.start()
+    for copy in loading[3:]:
+        copy.wait()
     loads = curv_ref.shape[0]
     width = 8
     matrix = curv_ref[...]
@@ -360,13 +405,23 @@
                     left[r] = left[r] - factors[j] * rows_left[j]
     alpha = jnp.concatenate(right, axis=0)
 
-    def mat_right(field):
-        return jnp.dot(
-            field, alpha, precision=lax.Precision.HIGHEST, preferred_element_type=jnp.float32
-        )
-
-    mult_ref[0, 0] = mat_right(precond_ref[...])
-    res_ref[0, 0] = residual_ref[...] - mat_right(image_ref[...])
+    high = alpha.astype(jnp.bfloat16)
+    low = (alpha - high.astype(jnp.float32)).astype(jnp.bfloat16)
+    parts = jnp.concatenate([high, low], axis=1)
+    parts = jnp.concatenate([parts, parts], axis=0)
+
+    def mat_right(pair):
+        both = dot(pair, parts)
+        return both[:, :loads] + both[:, loads:]
+
+    for copy in loading[:3]:
+        copy.wait()
+    mult_ref[...] = mat_right(precond_ref[...])
+    storing[0].start()
+    res_ref[...] = residual_ref[...] - mat_right(image_ref[...])
+    storing[1].start()
+    for copy in storing:
+        copy.wait()
 
 
 def shards(spans, chords, *args):
@@ -374,38 +429,45 @@
     size, loads = displacement.shape[2:]
     slots = link_rows.shape[3]
     tile = min(256, size)
-    steps = digits(spans)
+    (near, _), *steps = digits(spans)
     fans = sum(radix - 1 for radix, _ in steps)
-    sems = 2 * (chords - 1) + fans
-    chunk = loads // chords
+    group = chords * near
+    sems = 2 * (group - 1) + fans
+    chunk = loads // group
     f32, bf16 = jnp.float32, jnp.bfloat16
-    vmem = pl.BlockSpec(memory_space=pltpu.VMEM)
-    smem = pl.BlockSpec(memory_space=pltpu.SMEM)
+    hbm = pl.BlockSpec(memory_space=pltpu.HBM)
+    pair = jax.ShapeDtypeStruct((size, 2 * loads), bf16)
     field = jax.ShapeDtypeStruct((size, loads), f32)
     small = jax.ShapeDtypeStruct((loads, loads), f32)
     middle = pl.pallas_call(
         functools.partial(fields_kernel, spans, chords),
-        out_shape=(field, field, field, small, small),
-        in_specs=[vmem] * 7 + [smem],
-        out_specs=(vmem,) * 5,
-        scratch_shapes=[
+        out_shape=(pair, pair, field, small, small),
+        in_specs=[hbm] * 8,
+        out_specs=(hbm,) * 5,
+        scratch_shapes=[pltpu.VMEM(a.shape, a.dtype) for a in args]
+        + [
             pltpu.VMEM((size, size), bf16),
             pltpu.VMEM((size // tile, tile, tile), bf16),
             pltpu.VMEM((size // tile, tile, tile), bf16),
             pltpu.VMEM((3, 4, loads, slots), bf16),
             pltpu.VMEM((3, 4, loads, slots), bf16),
             pltpu.VMEM((2, loads, loads), f32),
-            pltpu.VMEM((2, chords - 1, chunk, loads), f32),
+            pltpu.VMEM((2, group - 1, chunk, loads), f32),
             pltpu.VMEM((2, len(steps) + 1, chunk, loads), f32),
-            pltpu.VMEM((2, fans, chunk, loads), f32),
+            pltpu.VMEM((2, max(fans, 1), chunk, loads), f32),
             pltpu.VMEM((2, loads, loads), f32),
             pltpu.SemaphoreType.DMA((3, 4)),
             pltpu.SemaphoreType.DMA((3, 4)),
             pltpu.SemaphoreType.DMA((2, sems)),
             pltpu.SemaphoreType.DMA((2, sems)),
+            pltpu.SemaphoreType.DMA((8,)),
+            pltpu.VMEM(pair.shape, pair.dtype),
+            pltpu.VMEM(pair.shape, pair.dtype),
+            pltpu.VMEM(field.shape, field.dtype),
+            pltpu.SemaphoreType.DMA((5,)),
         ],
         compiler_params=pltpu.CompilerParams(
-            collective_id=0, has_side_effects=True, vmem_limit_bytes=40 * 1024 * 1024
+            collective_id=0, has_side_effects=True, vmem_limit_bytes=60 * 1024 * 1024
         ),
         name="fields",
     )(*args)
@@ -413,9 +475,13 @@
     return pl.pallas_call(
         update_kernel,
         out_shape=(out, out),
-        in_specs=[vmem] * 5,
-        out_specs=(vmem, vmem),
-        compiler_params=pltpu.CompilerParams(vmem_limit_bytes=40 * 1024 * 1024),
+        in_specs=[hbm] * 5,
+        out_specs=(hbm, hbm),
+        scratch_shapes=[
+            pltpu.VMEM(a.shape, a.dtype) for a in (pair, pair, field, small, small, field, field)
+        ]
+        + [pltpu.SemaphoreType.DMA((5,)), pltpu.SemaphoreType.DMA((2,))],
+        compiler_params=pltpu.CompilerParams(vmem_limit_bytes=60 * 1024 * 1024),
         name="update",
     )(*middle)
 

time: 50.5 us -> 42.4 us (0.84)
  local copies, waits for them, and re-layouts: 6.62 us -> 0 us
  Pallas kernels: 42.9 us -> 41.6 us
    unnamed x16 -> x0, local copies, waits for them, and re-layouts: 6.62 us -> none
    pallas_call x1, Pallas kernels: 36.6 us -> 35.2 us  [shards(): pl.pallas_call(functools.partial(fields_kernel, spans, chords), out_shape...]
where the time goes in v2:
time: 42.4 us; the launch traced here: 42.2 us
  Pallas kernels  41.6 us (98%)
  between operations  0.64 us (2%)
    pallas_call x1, Pallas kernels, shards(): pl.pallas_call(functools.partial(fields_kernel, spans, chords), out_shape...  35.2 us
    pallas_call x1, Pallas kernels, shards(): pl.pallas_call(update_kernel, out_shape=(out, out), in_specs=[hbm] * 5, o...  6.39 us

profile of v2, /device:TPU:0, one launch (start us, length us, event | category | flops | bytes accessed | tf_op | source)
XLA Modules:
  0.0 42.2 jit_solution(16513933069386734651)
XLA Ops:
  0.6 35.2 %fields.1 = (bf16[1024,256]{1,0:T(8,128)(2,1)}, bf16[1024,256]{1,0:T(8,128)(2,1)}, f32[1024,128]{1,0:T(8,128)}, f32[128,128]{1,0:T(8,128)}, f32[128,128]{1,0:T(8,128)}) custom-call(bf16[1,1,1024,128]{3,2,1,0:T(8,128)(2,1)} %refs_0_.1, bf16[1,1,1024,1024]{3,2,1,0:T(8,128)(2,1)} %refs_1_.1, f32[1,1,1024]{2,1,0:T(1,128)} %refs_2_.1, f32[1,1,1024]{2,1,0:T(1,128)} %refs_3_.1, ...), custom_call_target="tpu_custom_call" | custom-call | tf_op jit(solution)/shard_map/fields/pallas_call | solution.py:442
  35.9 6.4 %update.1 = (f32[1,1,1024,128]{3,2,1,0:T(8,128)}, f32[1,1,1024,128]{3,2,1,0:T(8,128)}) custom-call(bf16[1024,256]{1,0:T(8,128)(2,1)} %get-tuple-element.7.refs_0_, bf16[1024,256]{1,0:T(8,128)(2,1)} %get-tuple-element.8.refs_1_, f32[1024,128]{1,0:T(8,128)} %get-tuple-element.9.refs_2_, f32[128,128]{1,0:T(8,128)} %get-tuple-element.10.refs_3_, ...), custom_call_target="tpu_custom_call" | custom-call | tf_op jit(solution)/shard_map/update/pallas_call | solution.py:475

commit v3 on v2

--- a/solution.py
+++ b/solution.py
@@ -65,6 +65,8 @@
     ) = refs
     size, loads = disp_ref.shape[2:]
     slots = rows_ref.shape[3]
+    half = sent.shape[3]
+    parts = loads // half
     tile = fdiag.shape[1]
     tiles = size // tile
     pos = {"span": lax.axis_index("span"), "chord": lax.axis_index("chord")}
@@ -121,42 +123,49 @@
         other = pos[axis] + step
         return jnp.logical_and(other >= 0, other < limit[axis])
 
-    def side_copy(e, d, slot):
+    def side_copy(e, h, d, slot):
         axis, step = SIDES[d]
         return pltpu.make_async_remote_copy(
-            src_ref=sent.at[e, d],
-            dst_ref=recv.at[e, slot],
-            send_sem=side_send.at[e, d],
-            recv_sem=side_recv.at[e, slot],
+            src_ref=sent.at[e, h, d],
+            dst_ref=recv.at[e, h, slot],
+            send_sem=side_send.at[e, h, d],
+            recv_sem=side_recv.at[e, h, slot],
             device_id={axis: pos[axis] + step},
             device_id_type=MESH,
         )
 
-    def send(e, term, scale=None):
+    def send(e, halves, term, scale=None):
         for pair in ((0, 1), (2, 3)):
             here = slice(pair[0] * slots, (pair[1] + 1) * slots)
             values = dot(term, hot[:, here])
             if scale is not None:
                 values = values * scale[:, here]
             values = values.astype(jnp.bfloat16)
-            for d in pair:
-                sent[e, d] = values[:, (d - pair[0]) * slots : (d - pair[0] + 1) * slots]
-
-                @pl.when(neighbour(d))
-                def _():
-                    side_copy(e, d, d ^ 1).start()
-
-    def partner(e):
+            for n, h in enumerate(halves):
+                for d in pair:
+                    sent[e, h, d] = values[
+                        n * half : (n + 1) * half,
+                        (d - pair[0]) * slots : (d - pair[0] + 1) * slots,
+                    ]
+
+                    @pl.when(neighbour(d))
+                    def _():
+                        side_copy(e, h, d, d ^ 1).start()
+
+    def partner(e, halves):
         total = 0
         for pair in ((2, 3), (0, 1)):
             for d in pair:
 
                 @pl.when(neighbour(d))
                 def _():
-                    side_copy(e, d, d).wait_recv()
-
-            values = jnp.concatenate([recv[e, d] for d in pair], axis=1)
-            total += dot_nt(values, hot[:, pair[0] * slots : (pair[1] + 1) * slots])
+                    for h in halves:
+                        side_copy(e, h, d, d).wait_recv()
+
+            values = [jnp.concatenate([recv[e, h, d] for d in pair], axis=1) for h in halves]
+            total += dot_nt(
+                jnp.concatenate(values, axis=0), hot[:, pair[0] * slots : (pair[1] + 1) * slots]
+            )
         return total.astype(jnp.bfloat16)
 
     def apply(diag_blocks, upper, scale, field):
@@ -286,10 +295,11 @@
         @pl.when(jnp.logical_not(neighbour(d)))
         def _():
             for e in range(3):
-                recv[e, d] = jnp.zeros(recv.shape[2:], recv.dtype)
+                for h in range(parts):
+                    recv[e, h, d] = jnp.zeros(recv.shape[3:], recv.dtype)
 
     pl.semaphore_wait(barrier, len(greeted))
-    send(0, disp.astype(jnp.bfloat16), slot_sign)
+    send(0, range(parts), disp.astype(jnp.bfloat16), slot_sign)
     signs = jnp.broadcast_to(slot_sign, (16, size)).astype(jnp.bfloat16)
     sign = dot_nt(signs, hot[...])[0:1, :]
     gap = (sign * disp).astype(jnp.bfloat16)
@@ -308,23 +318,30 @@
     fscale = fscale_ref[0]
     dscale = dscale_ref[0]
 
-    right = (gap, partner(0))
-    residual = total_of(right)
-    term = apply(ddiag, False, dscale, residual)
-    send(1, term)
-    residual_ref[...] = residual.T
+    def rows_of(pieces):
+        return tuple(jnp.concatenate([p[n] for p in pieces], axis=0) for n in range(2))
+
+    right, terms = [], []
+    for h in range(parts):
+        right.append((gap[h * half : (h + 1) * half], partner(0, (h,))))
+        terms.append(apply(ddiag, False, dscale, total_of(right[h])))
+        send(1, (h,), terms[h])
+    right = rows_of(right)
+    residual_ref[...] = total_of(right).T
     storing[2].start()
-    precond = (term, partner(1))
-    direction = total_of(precond)
+    precond, images = [], []
+    for h in range(parts):
+        precond.append((terms[h], partner(1, (h,))))
+        images.append(apply(fdiag, True, fscale, total_of(precond[h])))
+        send(2, (h,), images[h])
+    precond = rows_of(precond)
     gamma = Reduction(0)
     gamma.start(pair_gram(precond, right))
-    term = apply(fdiag, True, fscale, direction)
-    send(2, term)
-    gamma.advance()
     lay(precond_ref, precond)
     storing[0].start()
+    term = jnp.concatenate(images, axis=0)
     early = pair_gram(precond, (term,))
-    image = (term, partner(2))
+    image = (term, partner(2, range(parts)))
     curv = Reduction(1)
     curv.start(early + pair_gram(precond, image[1:]))
     gamma.advance()
@@ -343,7 +360,8 @@
 
             @pl.when(neighbour(d))
             def _():
-                side_copy(e, d, d).wait_send()
+                for h in range(parts):
+                    side_copy(e, h, d, d).wait_send()
 
     for copy in storing:
         copy.wait()
@@ -449,15 +467,15 @@
             pltpu.VMEM((size, size), bf16),
             pltpu.VMEM((size // tile, tile, tile), bf16),
             pltpu.VMEM((size // tile, tile, tile), bf16),
-            pltpu.VMEM((3, 4, loads, slots), bf16),
-            pltpu.VMEM((3, 4, loads, slots), bf16),
+            pltpu.VMEM((3, 2, 4, loads // 2, slots), bf16),
+            pltpu.VMEM((3, 2, 4, loads // 2, slots), bf16),
             pltpu.VMEM((2, loads, loads), f32),
             pltpu.VMEM((2, group - 1, chunk, loads), f32),
             pltpu.VMEM((2, len(steps) + 1, chunk, loads), f32),
             pltpu.VMEM((2, max(fans, 1), chunk, loads), f32),
             pltpu.VMEM((2, loads, loads), f32),
-            pltpu.SemaphoreType.DMA((3, 4)),
-            pltpu.SemaphoreType.DMA((3, 4)),
+            pltpu.SemaphoreType.DMA((3, 2, 4)),
+            pltpu.SemaphoreType.DMA((3, 2, 4)),
             pltpu.SemaphoreType.DMA((2, sems)),
             pltpu.SemaphoreType.DMA((2, sems)),
             pltpu.SemaphoreType.DMA((8,)),

time: 42.4 us -> 41.7 us (0.983)
  Pallas kernels: 41.6 us -> 40.9 us
    pallas_call x1, Pallas kernels: 35.2 us -> 34.5 us  [shards(): pl.pallas_call(functools.partial(fields_kernel, spans, chords), out_shape...]
where the time goes in v3:
time: 41.7 us; the launch traced here: 41.5 us
  Pallas kernels  40.9 us (98%)
  between operations  0.64 us (2%)
    pallas_call x1, Pallas kernels, shards(): pl.pallas_call(functools.partial(fields_kernel, spans, chords), out_shape...  34.5 us
    pallas_call x1, Pallas kernels, shards(): pl.pallas_call(update_kernel, out_shape=(out, out), in_specs=[hbm] * 5, o...  6.39 us

profile of v3, /device:TPU:0, one launch (start us, length us, event | category | flops | bytes accessed | tf_op | source)
XLA Modules:
  0.0 41.5 jit_solution(9789105410212089679)
XLA Ops:
  0.6 34.5 %fields.1 = (bf16[1024,256]{1,0:T(8,128)(2,1)}, bf16[1024,256]{1,0:T(8,128)(2,1)}, f32[1024,128]{1,0:T(8,128)}, f32[128,128]{1,0:T(8,128)}, f32[128,128]{1,0:T(8,128)}) custom-call(bf16[1,1,1024,128]{3,2,1,0:T(8,128)(2,1)} %refs_0_.1, bf16[1,1,1024,1024]{3,2,1,0:T(8,128)(2,1)} %refs_1_.1, f32[1,1,1024]{2,1,0:T(1,128)} %refs_2_.1, f32[1,1,1024]{2,1,0:T(1,128)} %refs_3_.1, ...), custom_call_target="tpu_custom_call" | custom-call | tf_op jit(solution)/shard_map/fields/pallas_call | solution.py:460
  35.1 6.4 %update.1 = (f32[1,1,1024,128]{3,2,1,0:T(8,128)}, f32[1,1,1024,128]{3,2,1,0:T(8,128)}) custom-call(bf16[1024,256]{1,0:T(8,128)(2,1)} %get-tuple-element.7.refs_0_, bf16[1024,256]{1,0:T(8,128)(2,1)} %get-tuple-element.8.refs_1_, f32[1024,128]{1,0:T(8,128)} %get-tuple-element.9.refs_2_, f32[128,128]{1,0:T(8,128)} %get-tuple-element.10.refs_3_, ...), custom_call_target="tpu_custom_call" | custom-call | tf_op jit(solution)/shard_map/update/pallas_call | solution.py:493

commit v4 on v3

--- a/solution.py
+++ b/solution.py
@@ -44,6 +44,8 @@
     disp_ref, packed_ref, fscale_ref, dscale_ref, diag_ref, rows_ref, signs_ref, counts_ref = local
     (
     hot,
+    spread,
+    mirrors,
     fdiag,
     ddiag,
     sent,
@@ -163,8 +165,8 @@
                         side_copy(e, h, d, d).wait_recv()
 
             values = [jnp.concatenate([recv[e, h, d] for d in pair], axis=1) for h in halves]
-            total += dot_nt(
-                jnp.concatenate(values, axis=0), hot[:, pair[0] * slots : (pair[1] + 1) * slots]
+            total += dot(
+                jnp.concatenate(values, axis=0), spread[pair[0] * slots : (pair[1] + 1) * slots]
             )
         return total.astype(jnp.bfloat16)
 
@@ -184,9 +186,9 @@
                     packed_ref[0, 0, direct[0] : direct[1], lo:hi],
                 )
             if mirrored[0] < mirrored[1]:
-                total += dot_nt(
+                total += dot(
                     operand[:, mirrored[0] : mirrored[1]],
-                    packed_ref[0, 0, lo:hi, mirrored[0] : mirrored[1]],
+                    mirrors[mirrored[0] : mirrored[1], lo:hi],
                 )
             out.append(total)
         product = jnp.concatenate(out, axis=1)
@@ -300,8 +302,15 @@
 
     pl.semaphore_wait(barrier, len(greeted))
     send(0, range(parts), disp.astype(jnp.bfloat16), slot_sign)
+    for d in range(4):
+        rows = jnp.broadcast_to(rows_ref[0, 0, d : d + 1, :], (8, slots)).astype(jnp.float32)
+        rows = rows.T.astype(jnp.int32)[:, 0:1]
+        row_ids = lax.broadcasted_iota(jnp.int32, (slots, size), 1)
+        spread[d * slots : (d + 1) * slots] = jnp.where(row_ids == rows, 1.0, 0.0).astype(
+            jnp.bfloat16
+        )
     signs = jnp.broadcast_to(slot_sign, (16, size)).astype(jnp.bfloat16)
-    sign = dot_nt(signs, hot[...])[0:1, :]
+    sign = dot(signs, spread[...])[0:1, :]
     gap = (sign * disp).astype(jnp.bfloat16)
     for n in (1, 2, 3, 4):
         loading[n].wait()
@@ -315,6 +324,14 @@
         lower = jnp.where(row_ids > col_ids, here, mirror)
         diag = diag_ref[0, :, lo:hi].astype(jnp.float32)
         ddiag[b] = jnp.where(row_ids == col_ids, diag, lower).astype(jnp.bfloat16)
+
+    def mirror_blocks(upper):
+        for b in range(tiles):
+            for a in range(b + 1, tiles) if upper else range(b):
+                ra, rb = slice(a * tile, (a + 1) * tile), slice(b * tile, (b + 1) * tile)
+                mirrors[ra, rb] = packed_ref[0, 0, rb, ra].T
+
+    mirror_blocks(False)
     fscale = fscale_ref[0]
     dscale = dscale_ref[0]
 
@@ -329,6 +346,7 @@
     right = rows_of(right)
     residual_ref[...] = total_of(right).T
     storing[2].start()
+    mirror_blocks(True)
     precond, images = [], []
     for h in range(parts):
         precond.append((terms[h], partner(1, (h,))))
@@ -464,6 +482,8 @@
         out_specs=(hbm,) * 5,
         scratch_shapes=[pltpu.VMEM(a.shape, a.dtype) for a in args]
         + [
+            pltpu.VMEM((size, size), bf16),
+            pltpu.VMEM((size, size), bf16),
             pltpu.VMEM((size, size), bf16),
             pltpu.VMEM((size // tile, tile, tile), bf16),
             pltpu.VMEM((size // tile, tile, tile), bf16),

time: 41.7 us -> 40.5 us (0.971)
  Pallas kernels: 40.9 us -> 39.7 us
    pallas_call x1, Pallas kernels: 34.5 us -> 33.3 us  [shards(): pl.pallas_call(functools.partial(fields_kernel, spans, chords), out_shape...]
where the time goes in v4:
time: 40.5 us; the launch traced here: 40.3 us
  Pallas kernels  39.7 us (98%)
  between operations  0.64 us (2%)
    pallas_call x1, Pallas kernels, shards(): pl.pallas_call(functools.partial(fields_kernel, spans, chords), out_shape...  33.3 us
    pallas_call x1, Pallas kernels, shards(): pl.pallas_call(update_kernel, out_shape=(out, out), in_specs=[hbm] * 5, o...  6.4 us

profile of v4, /device:TPU:0, one launch (start us, length us, event | category | flops | bytes accessed | tf_op | source)
XLA Modules:
  0.0 40.3 jit_solution(12028073560502177087)
XLA Ops:
  0.6 33.3 %fields.1 = (bf16[1024,256]{1,0:T(8,128)(2,1)}, bf16[1024,256]{1,0:T(8,128)(2,1)}, f32[1024,128]{1,0:T(8,128)}, f32[128,128]{1,0:T(8,128)}, f32[128,128]{1,0:T(8,128)}) custom-call(bf16[1,1,1024,128]{3,2,1,0:T(8,128)(2,1)} %refs_0_.1, bf16[1,1,1024,1024]{3,2,1,0:T(8,128)(2,1)} %refs_1_.1, f32[1,1,1024]{2,1,0:T(1,128)} %refs_2_.1, f32[1,1,1024]{2,1,0:T(1,128)} %refs_3_.1, ...), custom_call_target="tpu_custom_call" | custom-call | tf_op jit(solution)/shard_map/fields/pallas_call | solution.py:478
  33.9 6.4 %update.1 = (f32[1,1,1024,128]{3,2,1,0:T(8,128)}, f32[1,1,1024,128]{3,2,1,0:T(8,128)}) custom-call(bf16[1024,256]{1,0:T(8,128)(2,1)} %get-tuple-element.7.refs_0_, bf16[1024,256]{1,0:T(8,128)(2,1)} %get-tuple-element.8.refs_1_, f32[1024,128]{1,0:T(8,128)} %get-tuple-element.9.refs_2_, f32[128,128]{1,0:T(8,128)} %get-tuple-element.10.refs_3_, ...), custom_call_target="tpu_custom_call" | custom-call | tf_op jit(solution)/shard_map/update/pallas_call | solution.py:513
